TPU v7x, 256 devices: a whole 4x4x8 slice. The times are simulated.
256 devices in a mesh: gx: 8 (over y, core), gy: 8 (over z), gz: 4 (over x).
Axes of the slice: x: 4, y: 4, z: 8, core: 2. Of those that a mesh axis runs over, the one named last changes fastest.
Arguments:
- right_side: float32 [256, 256, 512], P('gx', 'gy', 'gz'), may hold values from -8 to 8
- coefficient: float32 [256, 256, 512], P('gx', 'gy', 'gz'), may hold values from 0.1 to 10
Outputs:
- fine_solution: float32 [256, 256, 512], P('gx', 'gy', 'gz')
- coarse_side: float32 [8, 8, 16], P('gx', 'gy', 'gz')
All inputs are finite; a program needn't handle non-finite values.
Results may differ from a plain program's by a relative error of at most 0.0001.
Values sent between devices are 32-bit elements; how exact they have to be, the bound alone decides.
A program may use at most 128 MiB of HBM per device.

v0:
```python
import jax
import jax.numpy as jnp
from jax import lax
from jax.experimental import pallas as pl
from jax.experimental.pallas import tpu as pltpu
from jax.sharding import PartitionSpec as P

MESH = pl.DeviceIdType.MESH
F32 = jnp.float32
GX, GY, GZ = 8, 8, 4
HX = 6
RO = 16
LOCAL = ((32, 32, 128), (16, 16, 64), (8, 8, 32))
OFFSETS = [
    (dx, dy, dz) for dz in (0, 1, -1) for dy in (0, 1, -1) for dx in (0, 1, -1)
    if (dx, dy, dz) != (0, 0, 0)
]
OFFSETS.sort(key=lambda o: abs(o[0]) + abs(o[1]) + abs(o[2]))


def lane_ids(rows):
    return lax.broadcasted_iota(jnp.int32, (rows, 128), 1)


def loop(lo, hi, step, body):
    assert (hi - lo) % step == 0
    def run(j, carry):
        body(lo + j * step)
        return carry
    lax.fori_loop(0, (hi - lo) // step, run, 0)


def zshift(values):
    rows = values[0].shape[0]
    down = [pltpu.roll(v, 1, 1) for v in values]
    up = [pltpu.roll(v, 127, 1) for v in values]
    if len(values) == 1:
        return down, up
    lane = lane_ids(rows)
    first, last = lane == 0, lane == 127
    zm = [jnp.where(first, down[1], down[0]), jnp.where(first, down[0], down[1])]
    zp = [jnp.where(last, up[1], up[0]), jnp.where(last, up[0], up[1])]
    return zm, zp


def coef_pass(K, work, cs, kcs, lo, hi, r0, r1, chunk, unroll):
    A, Q, D = work["A"], work["Q"], work["D"]

    def body(i0):
        for i in [i0 + u for u in range(unroll)]:
            for r in range(r0, r1, chunk):
                rows = pl.ds(r, chunk)
                ks = [K[i, kc, rows, :] for kc in kcs]
                zm, zp = zshift(ks)
                for n, (c, kc) in enumerate(zip(cs, kcs)):
                    k = ks[n]
                    g = [
                        k + K[i + 1, kc, rows, :],
                        k + K[i - 1, kc, rows, :],
                        k + K[i, kc, pl.ds(r + 1, chunk), :],
                        k + K[i, kc, pl.ds(r - 1, chunk), :],
                        k + zp[n],
                        k + zm[n],
                    ]
                    total = (g[0] + g[1]) + (g[2] + g[3]) + (g[4] + g[5])
                    inside = k > 0.0
                    q = jnp.where(inside, 0.8 / total, 0.0)
                    for j in range(6):
                        A[j, i, c, rows, :] = q * g[j]
                    Q[i, c, rows, :] = 2.0 * q
                    D[i, c, rows, :] = jnp.where(inside, 0.625 * total, 0.0)

    loop(lo, hi, unroll, body)


def first_pass(B, work, cs, kcs, lo, hi, r0, r1, unroll):
    Q, C = work["Q"], work["C"]
    rows = pl.ds(r0, r1 - r0)

    def body(i0):
        for i in [i0 + u for u in range(unroll)]:
            for c, kc in zip(cs, kcs):
                C[i, c, rows, :] = Q[i, c, rows, :] * B[i, kc, rows, :]

    loop(lo, hi, unroll, body)


def sweep(X, OUT, work, cs, lo, hi, r0, r1, chunk, unroll, resid):
    A, C, D = work["A"], work["C"], work["D"]

    def body(i0):
        for i in [i0 + u for u in range(unroll)]:
            for r in range(r0, r1, chunk):
                rows = pl.ds(r, chunk)
                vs = [X[i, c, rows, :] for c in cs]
                zm, zp = zshift(vs)
                for n, c in enumerate(cs):
                    s = A[0, i, c, rows, :] * X[i + 1, c, rows, :]
                    s = s + A[1, i, c, rows, :] * X[i - 1, c, rows, :]
                    t = A[2, i, c, rows, :] * X[i, c, pl.ds(r + 1, chunk), :]
                    t = t + A[3, i, c, rows, :] * X[i, c, pl.ds(r - 1, chunk), :]
                    u = A[4, i, c, rows, :] * zp[n] + A[5, i, c, rows, :] * zm[n]
                    total = C[i, c, rows, :] + (s + t) + u
                    if resid:
                        OUT[i, c, rows, :] = D[i, c, rows, :] * (total - 0.8 * vs[n])
                    else:
                        OUT[i, c, rows, :] = total + 0.2 * vs[n]

    loop(lo, hi, unroll, body)


def weights(nz, tile, full):
    lane = lax.broadcasted_iota(jnp.int32, (128, 128), 0)
    coarse = lax.broadcasted_iota(jnp.int32, (128, 128), 1)
    if nz == 128:
        z = lane if tile == 0 else jnp.where(lane < 64, lane + 128, lane - 128)
    else:
        z = jnp.where(lane >= 120, lane - 128, lane)
    delta = z - 2 * coarse
    used = coarse < nz // 2
    inner = used & (delta >= 0) & (delta <= 1)
    if not full:
        return jnp.where(inner, 0.125, 0.0).astype(F32)
    outer = used & ((delta == -1) | (delta == 2))
    return jnp.where(inner, 3.0 / 128.0, jnp.where(outer, 1.0 / 128.0, 0.0)).astype(F32)


def matmul(a, b):
    return jnp.dot(a, b, precision=lax.Precision.HIGHEST, preferred_element_type=F32)


def restrict(R, work, cs, n, base):
    nx, ny, nz = n
    T, S = work["T"], work["S"]
    hy = ny // 2
    lo, size = 8, ny + 16

    def body(I):
        rows = pl.ds(lo, size)
        for c in cs:
            p = base + 2 * I
            T[I, c, rows, :] = (R[p, c, rows, :] + R[p + 3, c, rows, :]) + 3.0 * (
                R[p + 1, c, rows, :] + R[p + 2, c, rows, :])

    loop(0, nx // 2, 1, body)

    def weigh(I, at):
        for m, c in enumerate(cs):
            e = [T[I, c, pl.ds(RO - 1 + j, hy, stride=2), :] for j in range(4)]
            S[m, at, :] = (e[0] + e[3]) + 3.0 * (e[1] + e[2])

    if hy % 8 == 0:
        loop(0, nx // 2, 1, lambda I: weigh(I, pl.ds(pl.multiple_of(I * hy, 8), hy)))
    else:
        for I in range(nx // 2):
            weigh(I, pl.ds(I * hy, hy))
    count = (nx // 2) * hy
    total = matmul(S[0, :count, :], weights(nz, 0, True))
    if len(cs) == 2:
        total = total + matmul(S[1, :count, :], weights(nz, 1, True))
    return total


def coarsen(K, work, n, base):
    nx, ny, nz = n
    T, S = work["T"], work["S"]
    hy = ny // 2
    rows = pl.ds(RO, ny)

    def body(I):
        T[I, 0, rows, :] = K[base + 2 * I, 0, rows, :] + K[base + 2 * I + 1, 0, rows, :]

    loop(0, nx // 2, 1, body)

    def weigh(I, at):
        e = [T[I, 0, pl.ds(RO + j, hy, stride=2), :] for j in range(2)]
        S[0, at, :] = e[0] + e[1]

    if hy % 8 == 0:
        loop(0, nx // 2, 1, lambda I: weigh(I, pl.ds(pl.multiple_of(I * hy, 8), hy)))
    else:
        for I in range(nx // 2):
            weigh(I, pl.ds(I * hy, hy))
    return matmul(S[0, : (nx // 2) * hy, :], weights(nz, 0, False))


def place(dst, value, n, base):
    nx, ny = n[0], n[1]
    for x in range(nx):
        dst[base + x, 0, pl.ds(RO, ny), :] = value[x * ny:(x + 1) * ny, :]


def pack_z(A, pack, n):
    nx, ny, nz = n
    gs = min(16, nx)
    lane = lane_ids(ny)

    def body(g):
        hi = jnp.zeros((ny, 128), F32)
        lo = jnp.zeros((ny, 128), F32)
        for x in range(gs):
            v = A[HX + g * gs + x, 0, pl.ds(RO, ny), :]
            here = (lane >= 8 * x) & (lane < 8 * x + 8)
            hi = jnp.where(here, pltpu.roll(v, (8 * x - nz + 8) % 128, 1), hi)
            lo = jnp.where(here, pltpu.roll(v, 8 * x, 1) if x else v, lo)
        pack[0, g, :, :] = hi
        pack[1, g, :, :] = lo

    loop(0, nx // gs, 1, body)


def unpack_z(A, got, n, keep_lo, keep_hi):
    nx, ny, nz = n
    gs = min(16, nx)
    rows = ny + 16
    lane = lane_ids(rows)
    start = nz % 128
    from_lo = (lane >= 120) & keep_lo
    from_hi = (lane >= start) & (lane < start + 8) & keep_hi

    def body(i):
        xe = i - HX + gs
        g = xe // gs
        at = lax.rem(xe, gs) * 8
        lo = pltpu.roll(got[0, g, :, :], 120 - at, 1)
        hi = pltpu.roll(got[1, g, :, :], lax.rem(start - at + 128, 128), 1)
        if nz == 128:
            own = jnp.zeros((rows, 128), F32)
            A[i, 1, pl.ds(8, rows), :] = jnp.where(from_lo, lo, jnp.where(from_hi, hi, own))
        else:
            own = A[i, 0, pl.ds(8, rows), :]
            A[i, 0, pl.ds(8, rows), :] = jnp.where(from_lo, lo, jnp.where(from_hi, hi, own))

    loop(0, nx + 2 * HX, 1, body)


def halo_copies(A, pack, got, ssem, rsem, n, me):
    nx, ny, _ = n
    gs = min(16, nx)
    ng = nx // gs
    xs = {0: (pl.ds(HX, nx), pl.ds(HX, nx)), 1: (pl.ds(nx, HX), pl.ds(0, HX)),
          -1: (pl.ds(HX, HX), pl.ds(nx + HX, HX))}
    ys = {0: (pl.ds(RO, ny), pl.ds(RO, ny)), 1: (pl.ds(RO + ny - 8, 8), pl.ds(8, 8)),
          -1: (pl.ds(RO, 8), pl.ds(RO + ny, 8))}
    gxs = {0: (pl.ds(0, ng), pl.ds(1, ng)), 1: (pl.ds(ng - 1, 1), pl.ds(0, 1)),
           -1: (pl.ds(0, 1), pl.ds(ng + 1, 1))}
    pys = {0: (pl.ds(0, ny), pl.ds(8, ny)), 1: (pl.ds(ny - 8, 8), pl.ds(0, 8)),
           -1: (pl.ds(0, 8), pl.ds(8 + ny, 8))}
    copies = []
    for j, (dx, dy, dz) in enumerate(OFFSETS):
        if dz == 0:
            src = A.at[xs[dx][0], 0, ys[dy][0], :]
            dst = A.at[xs[dx][1], 0, ys[dy][1], :]
        else:
            side = 0 if dz == 1 else 1
            src = pack.at[side, gxs[dx][0], pys[dy][0], :]
            dst = got.at[side, gxs[dx][1], pys[dy][1], :]
        copies.append(pltpu.make_async_remote_copy(
            src_ref=src, dst_ref=dst, send_sem=ssem.at[j], recv_sem=rsem.at[j],
            device_id=peer(me, (dx, dy, dz)), device_id_type=MESH))
    return copies


def peer(me, offset):
    return tuple(lax.rem(m + o + s, s) for m, o, s in zip(me, offset, (GX, GY, GZ)))


def start(copies):
    for copy in copies:
        copy.start()


def clear_outside(K, n, me):
    nx, ny, nz = n
    tiles = 2 if nz == 128 else 1

    def planes(first):
        K[pl.ds(first, HX), :, :, :] = jnp.zeros((HX, tiles, ny + 32, 128), F32)

    def rows(first):
        K[:, :, pl.ds(first, 8), :] = jnp.zeros((nx + 2 * HX, tiles, 8, 128), F32)

    pl.when(me[0] == 0)(lambda: planes(0))
    pl.when(me[0] == GX - 1)(lambda: planes(nx + HX))
    pl.when(me[1] == 0)(lambda: rows(8))
    pl.when(me[1] == GY - 1)(lambda: rows(RO + ny))


def kernel(b_hbm, k_hbm, fine_hbm, out_ref, K0, B0, K1, B1, K2, B2, K3, B3, K4, B4,
           A, Q, D, C, XA, XB, T, S, PS0, PR0, PS1, PR1, PS2, PR2, ZS, ZR, G, FIN,
           lsem, ssem, rsem, gssem, grsem):
    me = (lax.axis_index("gx"), lax.axis_index("gy"), lax.axis_index("gz"))
    gx, gy, gz = me
    work = {"A": A, "Q": Q, "D": D, "C": C, "T": T, "S": S}
    n0, n1, n2 = LOCAL
    keep_lo, keep_hi = gz > 0, gz < GZ - 1

    own = (pl.ds(HX, 32), 0, pl.ds(RO, 32), slice(None))
    load_k = pltpu.make_async_copy(k_hbm, K0.at[own], lsem.at[0])
    load_b = pltpu.make_async_copy(b_hbm, B0.at[own], lsem.at[1])
    load_k.start()
    load_b.start()

    partners = list(OFFSETS)
    partners += [(d, 0, 0) for d in range(2, GX - 1)]
    partners += [(0, d, 0) for d in range(2, GY - 1)]
    partners += [(0, 0, 2)]
    barrier = pltpu.get_barrier_semaphore()
    for offset in partners:
        pl.semaphore_signal(barrier, inc=1, device_id=peer(me, offset), device_id_type=MESH)

    load_k.wait()
    pack_z(K0, PS0.at[0], n0)
    pl.semaphore_wait(barrier, len(partners))
    k0 = halo_copies(K0, PS0.at[0], PR0.at[0], ssem.at[0], rsem.at[0], n0, me)
    start(k0)
    load_b.wait()
    pack_z(B0, PS0.at[1], n0)
    b0 = halo_copies(B0, PS0.at[1], PR0.at[1], ssem.at[1], rsem.at[1], n0, me)
    start(b0)

    def gather_copies(s):
        z = [pltpu.make_async_remote_copy(
            src_ref=ZS.at[s], dst_ref=ZR.at[s, o - 1], send_sem=gssem.at[s, o - 1],
            recv_sem=grsem.at[s, o - 1], device_id=peer(me, (0, 0, o)), device_id_type=MESH)
            for o in range(1, GZ)]
        y = [pltpu.make_async_remote_copy(
            src_ref=G.at[s, gx, gy], dst_ref=G.at[s, gx, gy], send_sem=gssem.at[s, 2 + o],
            recv_sem=grsem.at[s, 2 + o], device_id=peer(me, (0, o, 0)), device_id_type=MESH)
            for o in range(1, GY)]
        x = [pltpu.make_async_remote_copy(
            src_ref=G.at[s, gx], dst_ref=G.at[s, gx], send_sem=gssem.at[s, 9 + o],
            recv_sem=grsem.at[s, 9 + o], device_id=peer(me, (o, 0, 0)), device_id_type=MESH)
            for o in range(1, GX)]
        return z, y, x

    gk, gb = gather_copies(0), gather_copies(1)

    def gather_z(s, copies, rows):
        placed = pltpu.roll(rows, 16 * gz, 1)
        ZS[s, :, :] = placed[:8, :] + pltpu.roll(placed[8:, :], 64, 1)
        start(copies[0])

    def gather_y(s, copies):
        for copy in copies[0]:
            copy.wait_recv()
        G[s, gx, gy, :, :] = (ZS[s, :, :] + ZR[s, 0, :, :]) + (ZR[s, 1, :, :] + ZR[s, 2, :, :])
        start(copies[1])

    def gather_x(copies):
        for copy in copies[1]:
            copy.wait_recv()
        start(copies[2])

    def gather_end(s, copies, dst):
        for copy in copies[2]:
            copy.wait_recv()
        lower = lane_ids(4) < 64

        def body(g):
            for y in range(GY):
                for x in range(4):
                    v = G[s, g, y, pl.ds((x % 2) * 4, 4), :]
                    if x >= 2:
                        v = pltpu.roll(v, 64, 1)
                    dst[1 + 4 * g + x, 0, pl.ds(RO + 4 * y, 4), :] = jnp.where(lower, v, 0.0)

        loop(0, GX, 1, body)
        for group in copies:
            for copy in group:
                copy.wait_send()

    place(K1, coarsen(K0, work, n0, HX), n1, HX)
    pack_z(K1, PS1.at[0], n1)
    k1 = halo_copies(K1, PS1.at[0], PR1.at[0], ssem.at[2], rsem.at[2], n1, me)
    start(k1)
    place(K2, coarsen(K1, work, n1, HX), n2, HX)
    pack_z(K2, PS2.at[0], n2)
    k2 = halo_copies(K2, PS2.at[0], PR2.at[0], ssem.at[4], rsem.at[4], n2, me)
    start(k2)
    gather_z(0, gk, coarsen(K2, work, n2, HX))
    K3[...] = jnp.zeros(K3.shape, F32)
    K4[...] = jnp.zeros(K4.shape, F32)

    def land(copies, dst, got, n, is_k):
        for copy in copies:
            copy.wait_recv()
        for copy in copies:
            copy.wait_send()
        unpack_z(dst, got, n, keep_lo, keep_hi)
        if is_k:
            clear_outside(dst, n, me)

    def wide(n, K, B, cs, kcs, kc, bc, got, chunk, unroll):
        nx, ny, _ = n
        r0, r1 = 8, ny + 24
        land(kc, K, got.at[0], n, True)
        coef_pass(K, work, cs, kcs, 1, nx + 11, r0, r1, chunk, 1)
        land(bc, B, got.at[1], n, False)
        first_pass(B, work, cs, kcs, 1, nx + 11, r0, r1, 1)
        sweep(C, XA, work, cs, 2, nx + 10, r0, r1, chunk, unroll, False)
        sweep(XA, XB, work, cs, 3, nx + 9, r0, r1, chunk, unroll, False)
        sweep(XB, XA, work, cs, 4, nx + 8, r0, r1, chunk, unroll, False)

    def resid_wide(n, cs, chunk, unroll):
        nx, ny, _ = n
        sweep(XA, XB, work, cs, 5, nx + 7, 8, ny + 24, chunk, unroll, True)
        return restrict(XB, work, cs, n, HX - 1)

    wide(n0, K0, B0, (0, 1), (0, 1), k0, b0, PR0, 16, 1)
    store = pltpu.make_async_copy(XA.at[own], fine_hbm, lsem.at[2])
    store.start()
    gather_y(0, gk)
    place(B1, resid_wide(n0, (0, 1), 16, 1), n1, HX)
    pack_z(B1, PS1.at[1], n1)
    b1 = halo_copies(B1, PS1.at[1], PR1.at[1], ssem.at[3], rsem.at[3], n1, me)
    start(b1)
    store.wait()
    wide(n1, K1, B1, (0,), (0,), k1, b1, PR1, 32, 2)
    gather_x(gk)
    place(B2, resid_wide(n1, (0,), 32, 2), n2, HX)
    pack_z(B2, PS2.at[1], n2)
    b2 = halo_copies(B2, PS2.at[1], PR2.at[1], ssem.at[5], rsem.at[5], n2, me)
    start(b2)
    wide(n2, K2, B2, (0,), (0,), k2, b2, PR2, 24, 2)
    gather_z(1, gb, resid_wide(n2, (0,), 24, 2))

    n3, n4 = (32, 32, 64), (16, 16, 32)
    gather_end(0, gk, K3)
    gather_y(1, gb)

    def whole_prepare(n, K, c):
        nx, ny, _ = n
        for X in (C, XA, XB):
            for p in (0, nx + 1):
                X[p, c, pl.ds(8, ny + 16), :] = jnp.zeros((ny + 16, 128), F32)
            for r in (8, RO + ny):
                X[pl.ds(1, nx), c, pl.ds(r, 8), :] = jnp.zeros((nx, 8, 128), F32)
        coef_pass(K, work, (c,), (0,), 1, nx + 1, RO, RO + ny, ny, 1)

    def whole(n, B, c):
        nx, ny, _ = n
        span = (1, nx + 1, RO, RO + ny)
        first_pass(B, work, (c,), (0,), *span, 2)
        sweep(C, XA, work, (c,), *span, ny, 2, False)
        sweep(XA, XB, work, (c,), *span, ny, 2, False)
        sweep(XB, XA, work, (c,), *span, ny, 2, False)
        sweep(XA, XB, work, (c,), *span, ny, 2, True)
        return restrict(XB, work, (c,), n, 0)

    whole_prepare(n3, K3, 0)
    gather_x(gb)
    place(K4, coarsen(K3, work, n3, 1), n4, 1)
    whole_prepare(n4, K4, 1)
    gather_end(1, gb, B3)
    place(B4, whole(n3, B3, 0), n4, 1)
    FIN[...] = whole(n4, B4, 1)
    row = FIN[pl.ds(gx * 8 + gy, 1), :]
    out_ref[0, :, :] = pltpu.roll(row, lax.rem(128 - 4 * gz, 128), 1)[:, :4]


def local(right_side, coefficient):
    def vm(*shape):
        return pltpu.VMEM(shape, F32)

    dma = pltpu.SemaphoreType.DMA
    scratch = [
        vm(44, 2, 64, 128), vm(44, 2, 64, 128),
        vm(28, 1, 48, 128), vm(28, 1, 48, 128),
        vm(20, 1, 40, 128), vm(20, 1, 40, 128),
        vm(34, 1, 64, 128), vm(34, 1, 64, 128),
        vm(18, 1, 48, 128), vm(18, 1, 48, 128),
        vm(6, 44, 2, 64, 128),
    ] + [vm(44, 2, 64, 128) for _ in range(5)] + [
        vm(16, 2, 64, 128), vm(2, 256, 128),
        vm(2, 2, 2, 32, 128), vm(2, 2, 4, 48, 128),
        vm(2, 2, 1, 16, 128), vm(2, 2, 3, 32, 128),
        vm(2, 2, 1, 8, 128), vm(2, 2, 3, 24, 128),
        vm(2, 8, 128), vm(2, 3, 8, 128), vm(2, GX, GY, 8, 128), vm(64, 128),
        dma((3,)), dma((6, 26)), dma((6, 26)), dma((2, 17)), dma((2, 17)),
    ]
    hbm = pl.BlockSpec(memory_space=pl.ANY)
    return pl.pallas_call(
        kernel,
        out_shape=(
            jax.ShapeDtypeStruct(right_side.shape, F32),
            jax.ShapeDtypeStruct((1, 1, 4), F32),
        ),
        in_specs=[hbm, hbm],
        out_specs=(hbm, pl.BlockSpec(memory_space=pltpu.VMEM)),
        scratch_shapes=scratch,
        compiler_params=pltpu.CompilerParams(
            collective_id=0, has_side_effects=True, vmem_limit_bytes=56 * 2**20),
        name="down_leg",
    )(right_side, coefficient)


def solution(mesh):
    placed = (P("gx", "gy", "gz"), P("gx", "gy", "gz"))
    return jax.shard_map(
        local, mesh=mesh, in_specs=placed, out_specs=placed, check_vma=False)
```

profile of v0, /device:TPU:1, one launch (start us, length us, event | category | flops | bytes accessed | tf_op | source)
XLA Modules:
  0.0 102.2 jit_solution(14133006727026013564)
XLA Ops:
  0.6 99.1 %down_leg.1 = (f32[32,32,128]{2,1,0:T(8,128)}, f32[1,1,4]{2,1,0:T(1,128)}) custom-call(f32[32,32,128]{2,1,0:T(8,128)} %b_hbm.1, f32[32,32,128]{2,1,0:T(8,128)} %k_hbm.1), custom_call_target="tpu_custom_call" | custom-call | tf_op jit(solution)/shard_map/down_leg/pallas_call | solution.py:483
  99.8 0.0 copy-start
  99.8 1.9 %copy.6 = f32[32,32,128]{2,1,0:T(8,128)} copy(f32[32,32,128]{2,1,0:T(8,128)} %get-tuple-element.4) | data formatting | bytes 1048576
  101.7 0.0 copy-done
  101.7 0.5 copy.7
Async XLA Ops:
  99.8 1.9 %copy-start = (f32[1,1,4]{2,1,0:T(1,128)S(1)}, f32[1,1,4]{2,1,0:T(1,128)}, u32[]{:S(2)}) copy-start(f32[1,1,4]{2,1,0:T(1,128)} %get-tuple-element.5) | copy-start | bytes 52
where the time goes:
time: 102 us
  Pallas kernels  99.1 us (97%)
  local copies, waits for them, and re-layouts  2.38 us (2%)
    pallas_call x1, Pallas kernels, local(): pl.pallas_call(kernel, out_shape=(jax.ShapeDtypeStruct(right_side.shape,...  99.1 us
    unnamed x4, local copies, waits for them, and re-layouts  2.38 us

commit v1 on v0

--- a/solution.py
+++ b/solution.py
@@ -231,7 +231,7 @@
             own = A[i, 0, pl.ds(8, rows), :]
             A[i, 0, pl.ds(8, rows), :] = jnp.where(from_lo, lo, jnp.where(from_hi, hi, own))
 
-    loop(0, nx + 2 * HX, 1, body)
+    loop(0, nx + 2 * HX, 4, lambda i0: [body(i0 + u) for u in range(4)])
 
 
 def halo_copies(A, pack, got, ssem, rsem, n, me):
@@ -391,39 +391,39 @@
         if is_k:
             clear_outside(dst, n, me)
 
-    def wide(n, K, B, cs, kcs, kc, bc, got, chunk, unroll):
+    def wide(n, K, B, cs, kcs, kc, bc, got, chunk, steps):
         nx, ny, _ = n
         r0, r1 = 8, ny + 24
         land(kc, K, got.at[0], n, True)
-        coef_pass(K, work, cs, kcs, 1, nx + 11, r0, r1, chunk, 1)
+        coef_pass(K, work, cs, kcs, 1, nx + 11, r0, r1, chunk, steps[0])
         land(bc, B, got.at[1], n, False)
-        first_pass(B, work, cs, kcs, 1, nx + 11, r0, r1, 1)
-        sweep(C, XA, work, cs, 2, nx + 10, r0, r1, chunk, unroll, False)
-        sweep(XA, XB, work, cs, 3, nx + 9, r0, r1, chunk, unroll, False)
-        sweep(XB, XA, work, cs, 4, nx + 8, r0, r1, chunk, unroll, False)
-
-    def resid_wide(n, cs, chunk, unroll):
+        first_pass(B, work, cs, kcs, 1, nx + 11, r0, r1, steps[0])
+        sweep(C, XA, work, cs, 2, nx + 10, r0, r1, chunk, steps[1], False)
+        sweep(XA, XB, work, cs, 2, nx + 10, r0, r1, chunk, steps[1], False)
+        sweep(XB, XA, work, cs, 4, nx + 8, r0, r1, chunk, steps[2], False)
+
+    def resid_wide(n, cs, chunk, step):
         nx, ny, _ = n
-        sweep(XA, XB, work, cs, 5, nx + 7, 8, ny + 24, chunk, unroll, True)
+        sweep(XA, XB, work, cs, 4, nx + 8, 8, ny + 24, chunk, step, True)
         return restrict(XB, work, cs, n, HX - 1)
 
-    wide(n0, K0, B0, (0, 1), (0, 1), k0, b0, PR0, 16, 1)
+    wide(n0, K0, B0, (0, 1), (0, 1), k0, b0, PR0, 16, (6, 8, 9))
     store = pltpu.make_async_copy(XA.at[own], fine_hbm, lsem.at[2])
     store.start()
     gather_y(0, gk)
-    place(B1, resid_wide(n0, (0, 1), 16, 1), n1, HX)
+    place(B1, resid_wide(n0, (0, 1), 16, 9), n1, HX)
     pack_z(B1, PS1.at[1], n1)
     b1 = halo_copies(B1, PS1.at[1], PR1.at[1], ssem.at[3], rsem.at[3], n1, me)
     start(b1)
     store.wait()
-    wide(n1, K1, B1, (0,), (0,), k1, b1, PR1, 32, 2)
+    wide(n1, K1, B1, (0,), (0,), k1, b1, PR1, 32, (13, 8, 10))
     gather_x(gk)
-    place(B2, resid_wide(n1, (0,), 32, 2), n2, HX)
+    place(B2, resid_wide(n1, (0,), 32, 10), n2, HX)
     pack_z(B2, PS2.at[1], n2)
     b2 = halo_copies(B2, PS2.at[1], PR2.at[1], ssem.at[5], rsem.at[5], n2, me)
     start(b2)
-    wide(n2, K2, B2, (0,), (0,), k2, b2, PR2, 24, 2)
-    gather_z(1, gb, resid_wide(n2, (0,), 24, 2))
+    wide(n2, K2, B2, (0,), (0,), k2, b2, PR2, 24, (9, 8, 6))
+    gather_z(1, gb, resid_wide(n2, (0,), 24, 6))
 
     n3, n4 = (32, 32, 64), (16, 16, 32)
     gather_end(0, gk, K3)
@@ -436,16 +436,16 @@
                 X[p, c, pl.ds(8, ny + 16), :] = jnp.zeros((ny + 16, 128), F32)
             for r in (8, RO + ny):
                 X[pl.ds(1, nx), c, pl.ds(r, 8), :] = jnp.zeros((nx, 8, 128), F32)
-        coef_pass(K, work, (c,), (0,), 1, nx + 1, RO, RO + ny, ny, 1)
+        coef_pass(K, work, (c,), (0,), 1, nx + 1, RO, RO + ny, ny, 8)
 
     def whole(n, B, c):
         nx, ny, _ = n
         span = (1, nx + 1, RO, RO + ny)
-        first_pass(B, work, (c,), (0,), *span, 2)
-        sweep(C, XA, work, (c,), *span, ny, 2, False)
-        sweep(XA, XB, work, (c,), *span, ny, 2, False)
-        sweep(XB, XA, work, (c,), *span, ny, 2, False)
-        sweep(XA, XB, work, (c,), *span, ny, 2, True)
+        first_pass(B, work, (c,), (0,), *span, 8)
+        sweep(C, XA, work, (c,), *span, ny, 8, False)
+        sweep(XA, XB, work, (c,), *span, ny, 8, False)
+        sweep(XB, XA, work, (c,), *span, ny, 8, False)
+        sweep(XA, XB, work, (c,), *span, ny, 8, True)
         return restrict(XB, work, (c,), n, 0)
 
     whole_prepare(n3, K3, 0)

time: 102 us -> 75.7 us (0.74)
  Pallas kernels: 99.1 us -> 72.6 us
    pallas_call x1, Pallas kernels: 99.1 us -> 72.6 us  [local(): pl.pallas_call(kernel, out_shape=(jax.ShapeDtypeStruct(right_side.shape,...]
where the time goes in v1:
time: 75.7 us; the launch traced here: 75.6 us
  Pallas kernels  72.6 us (96%)
  local copies, waits for them, and re-layouts  2.38 us (3%)
    pallas_call x1, Pallas kernels, local(): pl.pallas_call(kernel, out_shape=(jax.ShapeDtypeStruct(right_side.shape,...  72.6 us
    unnamed x4, local copies, waits for them, and re-layouts  2.38 us

profile of v1, /device:TPU:1, one launch (start us, length us, event | category | flops | bytes accessed | tf_op | source)
XLA Modules:
  0.0 75.6 jit_solution(1134299927417169188)
XLA Ops:
  0.6 72.6 %down_leg.1 = (f32[32,32,128]{2,1,0:T(8,128)}, f32[1,1,4]{2,1,0:T(1,128)}) custom-call(f32[32,32,128]{2,1,0:T(8,128)} %b_hbm.1, f32[32,32,128]{2,1,0:T(8,128)} %k_hbm.1), custom_call_target="tpu_custom_call" | custom-call | tf_op jit(solution)/shard_map/down_leg/pallas_call | solution.py:483
  73.2 0.0 copy-start
  73.2 1.9 %copy.6 = f32[32,32,128]{2,1,0:T(8,128)} copy(f32[32,32,128]{2,1,0:T(8,128)} %get-tuple-element.4) | data formatting | bytes 1048576
  75.1 0.0 copy-done
  75.1 0.5 copy.7
Async XLA Ops:
  73.2 1.9 %copy-start = (f32[1,1,4]{2,1,0:T(1,128)S(1)}, f32[1,1,4]{2,1,0:T(1,128)}, u32[]{:S(2)}) copy-start(f32[1,1,4]{2,1,0:T(1,128)} %get-tuple-element.5) | copy-start | bytes 52

commit v2 on v1

--- a/solution.py
+++ b/solution.py
@@ -10,7 +10,7 @@
 GX, GY, GZ = 8, 8, 4
 HX = 6
 RO = 16
-LOCAL = ((32, 32, 128), (16, 16, 64), (8, 8, 32))
+LOCAL = ((32, 32, 128), (16, 16, 64), (8, 8, 128))
 OFFSETS = [
     (dx, dy, dz) for dz in (0, 1, -1) for dy in (0, 1, -1) for dx in (0, 1, -1)
     if (dx, dy, dz) != (0, 0, 0)
@@ -43,8 +43,10 @@
     return zm, zp
 
 
-def coef_pass(K, work, cs, kcs, lo, hi, r0, r1, chunk, unroll):
+def coef_pass(K, work, cs, kcs, lo, hi, r0, r1, chunk, unroll, line=False):
     A, Q, D = work["A"], work["Q"], work["D"]
+    lane = lane_ids(chunk)
+    first, last = lane == 0, lane == 127
 
     def body(i0):
         for i in [i0 + u for u in range(unroll)]:
@@ -52,6 +54,9 @@
                 rows = pl.ds(r, chunk)
                 ks = [K[i, kc, rows, :] for kc in kcs]
                 zm, zp = zshift(ks)
+                if line:
+                    zm = [jnp.where(first, 0.0, v) for v in zm]
+                    zp = [jnp.where(last, 0.0, v) for v in zp]
                 for n, (c, kc) in enumerate(zip(cs, kcs)):
                     k = ks[n]
                     g = [
@@ -65,8 +70,12 @@
                     total = (g[0] + g[1]) + (g[2] + g[3]) + (g[4] + g[5])
                     inside = k > 0.0
                     q = jnp.where(inside, 0.8 / total, 0.0)
+                    parts = [q * face for face in g]
+                    if line:
+                        parts[4] = jnp.where(last, 0.0, parts[4])
+                        parts[5] = jnp.where(first, 0.0, parts[5])
                     for j in range(6):
-                        A[j, i, c, rows, :] = q * g[j]
+                        A[j, i, c, rows, :] = parts[j]
                     Q[i, c, rows, :] = 2.0 * q
                     D[i, c, rows, :] = jnp.where(inside, 0.625 * total, 0.0)
 
@@ -231,7 +240,8 @@
             own = A[i, 0, pl.ds(8, rows), :]
             A[i, 0, pl.ds(8, rows), :] = jnp.where(from_lo, lo, jnp.where(from_hi, hi, own))
 
-    loop(0, nx + 2 * HX, 4, lambda i0: [body(i0 + u) for u in range(4)])
+    step = (nx + 2 * HX) // 4
+    loop(0, nx + 2 * HX, step, lambda i0: [body(i0 + u) for u in range(step)])
 
 
 def halo_copies(A, pack, got, ssem, rsem, n, me):
@@ -261,6 +271,53 @@
     return copies
 
 
+BLOCKS = [
+    (dx, dy, dz) for dz in (2, 1, 3, 0) for dy in (1, -1, 0) for dx in (1, -1, 0)
+    if (dx, dy, dz) != (0, 0, 0)
+]
+
+
+def dense_block(rows):
+    groups = []
+    for g in range(2):
+        parts = [rows[32 * g + 8 * j:32 * g + 8 * j + 8, :] for j in range(4)]
+        parts = [pltpu.roll(v, 32 * j, 1) if j else v for j, v in enumerate(parts)]
+        groups.append((parts[0] + parts[1]) + (parts[2] + parts[3]))
+    return groups
+
+
+def block_copies(N, s, ssem, rsem, me):
+    copies = []
+    for j, (dx, dy, dz) in enumerate(BLOCKS):
+        copies.append(pltpu.make_async_remote_copy(
+            src_ref=N.at[s, pl.ds(2, 2), 1, me[2]],
+            dst_ref=N.at[s, pl.ds(2 - 2 * dx, 2), 1 - dy, me[2]],
+            send_sem=ssem.at[s, j], recv_sem=rsem.at[s, j],
+            device_id=peer(me, (dx, dy, dz)), device_id_type=MESH))
+    return copies
+
+
+def assemble(N, s, dst):
+    lane = lane_ids(8)
+
+    def body(t):
+        for u in range(4):
+            j = (u + 2) % 4
+            g = t + (u + 2) // 4
+            for y in range(3):
+                parts = []
+                for z in range(GZ):
+                    v = N[s, g, y, z, :, :]
+                    turn = (32 * (z - j)) % 128
+                    parts.append(pltpu.roll(v, turn, 1) if turn else v)
+                dst[4 * t + u, 0, pl.ds(8 + 8 * y, 8), :] = jnp.where(
+                    lane < 64, jnp.where(lane < 32, parts[0], parts[1]),
+                    jnp.where(lane < 96, parts[2], parts[3]))
+
+    for t in range(5):
+        body(t)
+
+
 def peer(me, offset):
     return tuple(lax.rem(m + o + s, s) for m, o, s in zip(me, offset, (GX, GY, GZ)))
 
@@ -272,7 +329,7 @@
 
 def clear_outside(K, n, me):
     nx, ny, nz = n
-    tiles = 2 if nz == 128 else 1
+    tiles = 2 if nx == 32 else 1
 
     def planes(first):
         K[pl.ds(first, HX), :, :, :] = jnp.zeros((HX, tiles, ny + 32, 128), F32)
@@ -287,8 +344,8 @@
 
 
 def kernel(b_hbm, k_hbm, fine_hbm, out_ref, K0, B0, K1, B1, K2, B2, K3, B3, K4, B4,
-           A, Q, D, C, XA, XB, T, S, PS0, PR0, PS1, PR1, PS2, PR2, ZS, ZR, G, FIN,
-           lsem, ssem, rsem, gssem, grsem):
+           A, Q, D, C, XA, XB, T, S, PS0, PR0, PS1, PR1, N, G, FIN,
+           lsem, ssem, rsem, nssem, nrsem, gssem, grsem):
     me = (lax.axis_index("gx"), lax.axis_index("gy"), lax.axis_index("gz"))
     gx, gy, gz = me
     work = {"A": A, "Q": Q, "D": D, "C": C, "T": T, "S": S}
@@ -304,56 +361,48 @@
     partners = list(OFFSETS)
     partners += [(d, 0, 0) for d in range(2, GX - 1)]
     partners += [(0, d, 0) for d in range(2, GY - 1)]
-    partners += [(0, 0, 2)]
+    partners += [(dx, dy, 2) for dx in (-1, 0, 1) for dy in (-1, 0, 1)]
     barrier = pltpu.get_barrier_semaphore()
     for offset in partners:
         pl.semaphore_signal(barrier, inc=1, device_id=peer(me, offset), device_id_type=MESH)
 
     load_k.wait()
-    pack_z(K0, PS0.at[0], n0)
     pl.semaphore_wait(barrier, len(partners))
     k0 = halo_copies(K0, PS0.at[0], PR0.at[0], ssem.at[0], rsem.at[0], n0, me)
-    start(k0)
+    b0 = halo_copies(B0, PS0.at[1], PR0.at[1], ssem.at[1], rsem.at[1], n0, me)
+    flat = [o[2] == 0 for o in OFFSETS]
+    start([c for c, f in zip(k0, flat) if f])
+    pack_z(K0, PS0.at[0], n0)
+    start([c for c, f in zip(k0, flat) if not f])
     load_b.wait()
+    start([c for c, f in zip(b0, flat) if f])
     pack_z(B0, PS0.at[1], n0)
-    b0 = halo_copies(B0, PS0.at[1], PR0.at[1], ssem.at[1], rsem.at[1], n0, me)
-    start(b0)
+    start([c for c, f in zip(b0, flat) if not f])
 
     def gather_copies(s):
-        z = [pltpu.make_async_remote_copy(
-            src_ref=ZS.at[s], dst_ref=ZR.at[s, o - 1], send_sem=gssem.at[s, o - 1],
-            recv_sem=grsem.at[s, o - 1], device_id=peer(me, (0, 0, o)), device_id_type=MESH)
-            for o in range(1, GZ)]
         y = [pltpu.make_async_remote_copy(
-            src_ref=G.at[s, gx, gy], dst_ref=G.at[s, gx, gy], send_sem=gssem.at[s, 2 + o],
-            recv_sem=grsem.at[s, 2 + o], device_id=peer(me, (0, o, 0)), device_id_type=MESH)
-            for o in range(1, GY)]
+            src_ref=G.at[s, gx, gy], dst_ref=G.at[s, gx, gy], send_sem=gssem.at[s, o - 1],
+            recv_sem=grsem.at[s, o - 1], device_id=peer(me, (0, o, 0)), device_id_type=MESH)
+            for o in (4, 3, 5, 2, 6, 1, 7)]
         x = [pltpu.make_async_remote_copy(
-            src_ref=G.at[s, gx], dst_ref=G.at[s, gx], send_sem=gssem.at[s, 9 + o],
-            recv_sem=grsem.at[s, 9 + o], device_id=peer(me, (o, 0, 0)), device_id_type=MESH)
-            for o in range(1, GX)]
-        return z, y, x
+            src_ref=G.at[s, gx], dst_ref=G.at[s, gx], send_sem=gssem.at[s, 6 + o],
+            recv_sem=grsem.at[s, 6 + o], device_id=peer(me, (o, 0, 0)), device_id_type=MESH)
+            for o in (4, 3, 5, 2, 6, 1, 7)]
+        return y, x
 
     gk, gb = gather_copies(0), gather_copies(1)
 
-    def gather_z(s, copies, rows):
-        placed = pltpu.roll(rows, 16 * gz, 1)
-        ZS[s, :, :] = placed[:8, :] + pltpu.roll(placed[8:, :], 64, 1)
+    def gather_y(s, copies, rows):
+        G[s, gx, gy, :, :] = rows[:8, :] + pltpu.roll(rows[8:, :], 64, 1)
         start(copies[0])
 
-    def gather_y(s, copies):
+    def gather_x(copies):
         for copy in copies[0]:
             copy.wait_recv()
-        G[s, gx, gy, :, :] = (ZS[s, :, :] + ZR[s, 0, :, :]) + (ZR[s, 1, :, :] + ZR[s, 2, :, :])
         start(copies[1])
 
-    def gather_x(copies):
+    def gather_end(s, copies, dst):
         for copy in copies[1]:
-            copy.wait_recv()
-        start(copies[2])
-
-    def gather_end(s, copies, dst):
-        for copy in copies[2]:
             copy.wait_recv()
         lower = lane_ids(4) < 64
 
@@ -374,11 +423,19 @@
     pack_z(K1, PS1.at[0], n1)
     k1 = halo_copies(K1, PS1.at[0], PR1.at[0], ssem.at[2], rsem.at[2], n1, me)
     start(k1)
-    place(K2, coarsen(K1, work, n1, HX), n2, HX)
-    pack_z(K2, PS2.at[0], n2)
-    k2 = halo_copies(K2, PS2.at[0], PR2.at[0], ssem.at[4], rsem.at[4], n2, me)
-    start(k2)
-    gather_z(0, gk, coarsen(K2, work, n2, HX))
+    def send_block(s, rows):
+        for g, v in enumerate(dense_block(rows)):
+            N[s, 2 + g, 1, gz, :, :] = v
+        copies = block_copies(N, s, nssem, nrsem, me)
+        start(copies)
+        return copies
+
+    def land_block(s, copies, dst):
+        for copy in copies:
+            copy.wait_recv()
+        assemble(N, s, dst)
+
+    k2 = send_block(0, coarsen(K1, work, n1, HX))
     K3[...] = jnp.zeros(K3.shape, F32)
     K4[...] = jnp.zeros(K4.shape, F32)
 
@@ -391,13 +448,14 @@
         if is_k:
             clear_outside(dst, n, me)
 
-    def wide(n, K, B, cs, kcs, kc, bc, got, chunk, steps):
+    def coefs(n, K, cs, chunk, step, line=False):
+        nx, ny, _ = n
+        coef_pass(K, work, cs, cs, 1, nx + 11, 8, ny + 24, chunk, step, line)
+
+    def sweeps(n, B, cs, chunk, steps):
         nx, ny, _ = n
         r0, r1 = 8, ny + 24
-        land(kc, K, got.at[0], n, True)
-        coef_pass(K, work, cs, kcs, 1, nx + 11, r0, r1, chunk, steps[0])
-        land(bc, B, got.at[1], n, False)
-        first_pass(B, work, cs, kcs, 1, nx + 11, r0, r1, steps[0])
+        first_pass(B, work, cs, cs, 1, nx + 11, r0, r1, steps[0])
         sweep(C, XA, work, cs, 2, nx + 10, r0, r1, chunk, steps[1], False)
         sweep(XA, XB, work, cs, 2, nx + 10, r0, r1, chunk, steps[1], False)
         sweep(XB, XA, work, cs, 4, nx + 8, r0, r1, chunk, steps[2], False)
@@ -407,27 +465,35 @@
         sweep(XA, XB, work, cs, 4, nx + 8, 8, ny + 24, chunk, step, True)
         return restrict(XB, work, cs, n, HX - 1)
 
-    wide(n0, K0, B0, (0, 1), (0, 1), k0, b0, PR0, 16, (6, 8, 9))
+    land(k0, K0, PR0.at[0], n0, True)
+    coefs(n0, K0, (0, 1), 16, 6)
+    land(b0, B0, PR0.at[1], n0, False)
+    sweeps(n0, B0, (0, 1), 16, (6, 8, 9))
     store = pltpu.make_async_copy(XA.at[own], fine_hbm, lsem.at[2])
     store.start()
-    gather_y(0, gk)
     place(B1, resid_wide(n0, (0, 1), 16, 9), n1, HX)
     pack_z(B1, PS1.at[1], n1)
     b1 = halo_copies(B1, PS1.at[1], PR1.at[1], ssem.at[3], rsem.at[3], n1, me)
     start(b1)
     store.wait()
-    wide(n1, K1, B1, (0,), (0,), k1, b1, PR1, 32, (13, 8, 10))
+    land(k1, K1, PR1.at[0], n1, True)
+    coefs(n1, K1, (0,), 32, 13)
+    land_block(0, k2, K2)
+    clear_outside(K2, n2, me)
+    gather_y(0, gk, coarsen(K2, work, n2, HX))
+    land(b1, B1, PR1.at[1], n1, False)
+    sweeps(n1, B1, (0,), 32, (13, 8, 10))
+    b2 = send_block(1, resid_wide(n1, (0,), 32, 10))
+    coefs(n2, K2, (0,), 24, 9, True)
     gather_x(gk)
-    place(B2, resid_wide(n1, (0,), 32, 10), n2, HX)
-    pack_z(B2, PS2.at[1], n2)
-    b2 = halo_copies(B2, PS2.at[1], PR2.at[1], ssem.at[5], rsem.at[5], n2, me)
-    start(b2)
-    wide(n2, K2, B2, (0,), (0,), k2, b2, PR2, 24, (9, 8, 6))
-    gather_z(1, gb, resid_wide(n2, (0,), 24, 6))
+    land_block(1, b2, B2)
+    sweeps(n2, B2, (0,), 24, (9, 8, 6))
+    gather_y(1, gb, resid_wide(n2, (0,), 24, 6))
+    for copy in k2 + b2:
+        copy.wait_send()
 
     n3, n4 = (32, 32, 64), (16, 16, 32)
     gather_end(0, gk, K3)
-    gather_y(1, gb)
 
     def whole_prepare(n, K, c):
         nx, ny, _ = n
@@ -436,16 +502,16 @@
                 X[p, c, pl.ds(8, ny + 16), :] = jnp.zeros((ny + 16, 128), F32)
             for r in (8, RO + ny):
                 X[pl.ds(1, nx), c, pl.ds(r, 8), :] = jnp.zeros((nx, 8, 128), F32)
-        coef_pass(K, work, (c,), (0,), 1, nx + 1, RO, RO + ny, ny, 8)
+        coef_pass(K, work, (c,), (0,), 1, nx + 1, RO, RO + ny, ny, 16)
 
     def whole(n, B, c):
         nx, ny, _ = n
         span = (1, nx + 1, RO, RO + ny)
-        first_pass(B, work, (c,), (0,), *span, 8)
-        sweep(C, XA, work, (c,), *span, ny, 8, False)
-        sweep(XA, XB, work, (c,), *span, ny, 8, False)
-        sweep(XB, XA, work, (c,), *span, ny, 8, False)
-        sweep(XA, XB, work, (c,), *span, ny, 8, True)
+        first_pass(B, work, (c,), (0,), *span, 16)
+        sweep(C, XA, work, (c,), *span, ny, 16, False)
+        sweep(XA, XB, work, (c,), *span, ny, 16, False)
+        sweep(XB, XA, work, (c,), *span, ny, 16, False)
+        sweep(XA, XB, work, (c,), *span, ny, 16, True)
         return restrict(XB, work, (c,), n, 0)
 
     whole_prepare(n3, K3, 0)
@@ -457,6 +523,21 @@
     FIN[...] = whole(n4, B4, 1)
     row = FIN[pl.ds(gx * 8 + gy, 1), :]
     out_ref[0, :, :] = pltpu.roll(row, lax.rem(128 - 4 * gz, 128), 1)[:, :4]
+
+
+def finish(fine, coarse, fine_out, coarse_out, buf, small, isem, osem):
+    loads = [pltpu.make_async_copy(coarse, small, isem.at[4])]
+    stores = [pltpu.make_async_copy(small, coarse_out, osem.at[4])]
+    for j in range(4):
+        part = pl.ds(8 * j, 8)
+        loads.append(pltpu.make_async_copy(fine.at[part], buf.at[part], isem.at[j]))
+        stores.append(pltpu.make_async_copy(buf.at[part], fine_out.at[part], osem.at[j]))
+    start(loads)
+    for load, store in zip(loads, stores):
+        load.wait()
+        store.start()
+    for store in stores:
+        store.wait()
 
 
 def local(right_side, coefficient):
@@ -475,12 +556,11 @@
         vm(16, 2, 64, 128), vm(2, 256, 128),
         vm(2, 2, 2, 32, 128), vm(2, 2, 4, 48, 128),
         vm(2, 2, 1, 16, 128), vm(2, 2, 3, 32, 128),
-        vm(2, 2, 1, 8, 128), vm(2, 2, 3, 24, 128),
-        vm(2, 8, 128), vm(2, 3, 8, 128), vm(2, GX, GY, 8, 128), vm(64, 128),
-        dma((3,)), dma((6, 26)), dma((6, 26)), dma((2, 17)), dma((2, 17)),
+        vm(2, 6, 3, GZ, 8, 128), vm(2, GX, GY, 8, 128), vm(64, 128),
+        dma((3,)), dma((4, 26)), dma((4, 26)), dma((2, 35)), dma((2, 35)), dma((2, 14)), dma((2, 14)),
     ]
     hbm = pl.BlockSpec(memory_space=pl.ANY)
-    return pl.pallas_call(
+    fine, coarse = pl.pallas_call(
         kernel,
         out_shape=(
             jax.ShapeDtypeStruct(right_side.shape, F32),
@@ -494,6 +574,19 @@
         name="down_leg",
     )(right_side, coefficient)
 
+    return pl.pallas_call(
+        finish,
+        out_shape=(
+            jax.ShapeDtypeStruct(right_side.shape, F32),
+            jax.ShapeDtypeStruct((1, 1, 4), F32),
+        ),
+        in_specs=[hbm, hbm],
+        out_specs=(hbm, hbm),
+        scratch_shapes=[vm(32, 32, 128), vm(1, 1, 4), dma((5,)), dma((5,))],
+        compiler_params=pltpu.CompilerParams(vmem_limit_bytes=60 * 2**20),
+        name="finish",
+    )(fine, coarse)
+
 
 def solution(mesh):
     placed = (P("gx", "gy", "gz"), P("gx", "gy", "gz"))

time: 75.7 us -> 69.7 us (0.921)
  Pallas kernels: 72.6 us -> 68.9 us
  local copies, waits for them, and re-layouts: 2.38 us -> 0 us
    pallas_call x1, Pallas kernels: 72.6 us -> 67.1 us  [local(): pl.pallas_call(kernel, out_shape=(jax.ShapeDtypeStruct(right_side.shape,...]
    unnamed x4 -> x0, local copies, waits for them, and re-layouts: 2.38 us -> none
    pallas_call x0 -> x1, Pallas kernels: none -> 1.84 us  [local(): pl.pallas_call(finish, out_shape=(jax.ShapeDtypeStruct(right_side.shape,...]
where the time goes in v2:
time: 69.7 us; the launch traced here: 69.6 us
  Pallas kernels  68.9 us (99%)
    pallas_call x1, Pallas kernels, local(): pl.pallas_call(kernel, out_shape=(jax.ShapeDtypeStruct(right_side.shape,...  67.1 us
    pallas_call x1, Pallas kernels, local(): pl.pallas_call(finish, out_shape=(jax.ShapeDtypeStruct(right_side.shape,...  1.84 us

profile of v2, /device:TPU:1, one launch (start us, length us, event | category | flops | bytes accessed | tf_op | source)
XLA Modules:
  0.0 69.6 jit_solution(9684148442073621876)
XLA Ops:
  0.6 67.1 %down_leg.1 = (f32[32,32,128]{2,1,0:T(8,128)}, f32[1,1,4]{2,1,0:T(1,128)}) custom-call(f32[32,32,128]{2,1,0:T(8,128)} %b_hbm.1, f32[32,32,128]{2,1,0:T(8,128)} %k_hbm.1), custom_call_target="tpu_custom_call" | custom-call | tf_op jit(solution)/shard_map/down_leg/pallas_call | solution.py:563
  67.7 1.8 %finish.1 = (f32[32,32,128]{2,1,0:T(8,128)}, f32[1,1,4]{2,1,0:T(1,128)}) custom-call(f32[32,32,128]{2,1,0:T(8,128)} %get-tuple-element.4.fine, f32[1,1,4]{2,1,0:T(1,128)} %get-tuple-element.5.coarse), custom_call_target="tpu_custom_call" | custom-call | tf_op jit(solution)/shard_map/finish/pallas_call | solution.py:577

commit v3 on v2

--- a/solution.py
+++ b/solution.py
@@ -151,7 +151,7 @@
             T[I, c, rows, :] = (R[p, c, rows, :] + R[p + 3, c, rows, :]) + 3.0 * (
                 R[p + 1, c, rows, :] + R[p + 2, c, rows, :])
 
-    loop(0, nx // 2, 1, body)
+    loop(0, nx // 2, 4, lambda i0: [body(i0 + u) for u in range(4)])
 
     def weigh(I, at):
         for m, c in enumerate(cs):
@@ -159,7 +159,8 @@
             S[m, at, :] = (e[0] + e[3]) + 3.0 * (e[1] + e[2])
 
     if hy % 8 == 0:
-        loop(0, nx // 2, 1, lambda I: weigh(I, pl.ds(pl.multiple_of(I * hy, 8), hy)))
+        loop(0, nx // 2, 4, lambda i0: [
+            weigh(i0 + u, pl.ds(pl.multiple_of((i0 + u) * hy, 8), hy)) for u in range(4)])
     else:
         for I in range(nx // 2):
             weigh(I, pl.ds(I * hy, hy))
@@ -179,14 +180,15 @@
     def body(I):
         T[I, 0, rows, :] = K[base + 2 * I, 0, rows, :] + K[base + 2 * I + 1, 0, rows, :]
 
-    loop(0, nx // 2, 1, body)
+    loop(0, nx // 2, 4, lambda i0: [body(i0 + u) for u in range(4)])
 
     def weigh(I, at):
         e = [T[I, 0, pl.ds(RO + j, hy, stride=2), :] for j in range(2)]
         S[0, at, :] = e[0] + e[1]
 
     if hy % 8 == 0:
-        loop(0, nx // 2, 1, lambda I: weigh(I, pl.ds(pl.multiple_of(I * hy, 8), hy)))
+        loop(0, nx // 2, 4, lambda i0: [
+            weigh(i0 + u, pl.ds(pl.multiple_of((i0 + u) * hy, 8), hy)) for u in range(4)])
     else:
         for I in range(nx // 2):
             weigh(I, pl.ds(I * hy, hy))
@@ -404,17 +406,19 @@
     def gather_end(s, copies, dst):
         for copy in copies[1]:
             copy.wait_recv()
-        lower = lane_ids(4) < 64
+        lower = lane_ids(8) < 64
+        top = lax.broadcasted_iota(jnp.int32, (8, 128), 0) < 4
 
         def body(g):
-            for y in range(GY):
-                for x in range(4):
-                    v = G[s, g, y, pl.ds((x % 2) * 4, 4), :]
-                    if x >= 2:
-                        v = pltpu.roll(v, 64, 1)
-                    dst[1 + 4 * g + x, 0, pl.ds(RO + 4 * y, 4), :] = jnp.where(lower, v, 0.0)
-
-        loop(0, GX, 1, body)
+            for m in range(GY // 2):
+                a, b = G[s, g, 2 * m, :, :], G[s, g, 2 * m + 1, :, :]
+                first = jnp.where(top, a, pltpu.roll(b, 4, 0))
+                second = jnp.where(top, pltpu.roll(a, 4, 0), b)
+                planes = (first, second, pltpu.roll(first, 64, 1), pltpu.roll(second, 64, 1))
+                for p, v in enumerate(planes):
+                    dst[1 + 4 * g + p, 0, pl.ds(RO + 8 * m, 8), :] = jnp.where(lower, v, 0.0)
+
+        loop(0, GX, 2, lambda g: (body(g), body(g + 1)))
         for group in copies:
             for copy in group:
                 copy.wait_send()
@@ -462,16 +466,16 @@
 
     def resid_wide(n, cs, chunk, step):
         nx, ny, _ = n
-        sweep(XA, XB, work, cs, 4, nx + 8, 8, ny + 24, chunk, step, True)
+        sweep(XA, XB, work, cs, 5, nx + 7, 8, ny + 24, chunk, step, True)
         return restrict(XB, work, cs, n, HX - 1)
 
     land(k0, K0, PR0.at[0], n0, True)
     coefs(n0, K0, (0, 1), 16, 6)
     land(b0, B0, PR0.at[1], n0, False)
-    sweeps(n0, B0, (0, 1), 16, (6, 8, 9))
+    sweeps(n0, B0, (0, 1), 16, (6, 10, 18))
     store = pltpu.make_async_copy(XA.at[own], fine_hbm, lsem.at[2])
     store.start()
-    place(B1, resid_wide(n0, (0, 1), 16, 9), n1, HX)
+    place(B1, resid_wide(n0, (0, 1), 16, 17), n1, HX)
     pack_z(B1, PS1.at[1], n1)
     b1 = halo_copies(B1, PS1.at[1], PR1.at[1], ssem.at[3], rsem.at[3], n1, me)
     start(b1)
@@ -482,13 +486,13 @@
     clear_outside(K2, n2, me)
     gather_y(0, gk, coarsen(K2, work, n2, HX))
     land(b1, B1, PR1.at[1], n1, False)
-    sweeps(n1, B1, (0,), 32, (13, 8, 10))
-    b2 = send_block(1, resid_wide(n1, (0,), 32, 10))
+    sweeps(n1, B1, (0,), 32, (13, 12, 10))
+    b2 = send_block(1, resid_wide(n1, (0,), 32, 9))
     coefs(n2, K2, (0,), 24, 9, True)
     gather_x(gk)
     land_block(1, b2, B2)
     sweeps(n2, B2, (0,), 24, (9, 8, 6))
-    gather_y(1, gb, resid_wide(n2, (0,), 24, 6))
+    gather_y(1, gb, resid_wide(n2, (0,), 24, 5))
     for copy in k2 + b2:
         copy.wait_send()
 

time: 69.7 us -> 68.1 us (0.977)
  Pallas kernels: 68.9 us -> 67.4 us
    pallas_call x1, Pallas kernels: 67.1 us -> 65.5 us  [local(): pl.pallas_call(kernel, out_shape=(jax.ShapeDtypeStruct(right_side.shape,...]
where the time goes in v3:
time: 68.1 us; the launch traced here: 68 us
  Pallas kernels  67.4 us (99%)
    pallas_call x1, Pallas kernels, local(): pl.pallas_call(kernel, out_shape=(jax.ShapeDtypeStruct(right_side.shape,...  65.5 us
    pallas_call x1, Pallas kernels, local(): pl.pallas_call(finish, out_shape=(jax.ShapeDtypeStruct(right_side.shape,...  1.84 us

profile of v3, /device:TPU:1, one launch (start us, length us, event | category | flops | bytes accessed | tf_op | source)
XLA Modules:
  0.0 68.0 jit_solution(18108675395756216770)
XLA Ops:
  0.6 65.5 %down_leg.1 = (f32[32,32,128]{2,1,0:T(8,128)}, f32[1,1,4]{2,1,0:T(1,128)}) custom-call(f32[32,32,128]{2,1,0:T(8,128)} %b_hbm.1, f32[32,32,128]{2,1,0:T(8,128)} %k_hbm.1), custom_call_target="tpu_custom_call" | custom-call | tf_op jit(solution)/shard_map/down_leg/pallas_call | solution.py:567
  66.2 1.8 %finish.1 = (f32[32,32,128]{2,1,0:T(8,128)}, f32[1,1,4]{2,1,0:T(1,128)}) custom-call(f32[32,32,128]{2,1,0:T(8,128)} %get-tuple-element.4.fine, f32[1,1,4]{2,1,0:T(1,128)} %get-tuple-element.5.coarse), custom_call_target="tpu_custom_call" | custom-call | tf_op jit(solution)/shard_map/finish/pallas_call | solution.py:581

commit v4 on v3

--- a/solution.py
+++ b/solution.py
@@ -246,12 +246,12 @@
     loop(0, nx + 2 * HX, step, lambda i0: [body(i0 + u) for u in range(step)])
 
 
-def halo_copies(A, pack, got, ssem, rsem, n, me):
+def halo_copies(A, pack, got, ssem, rsem, n, me, w=HX):
     nx, ny, _ = n
     gs = min(16, nx)
     ng = nx // gs
-    xs = {0: (pl.ds(HX, nx), pl.ds(HX, nx)), 1: (pl.ds(nx, HX), pl.ds(0, HX)),
-          -1: (pl.ds(HX, HX), pl.ds(nx + HX, HX))}
+    xs = {0: (pl.ds(HX, nx), pl.ds(HX, nx)), 1: (pl.ds(HX + nx - w, w), pl.ds(HX - w, w)),
+          -1: (pl.ds(HX, w), pl.ds(nx + HX, w))}
     ys = {0: (pl.ds(RO, ny), pl.ds(RO, ny)), 1: (pl.ds(RO + ny - 8, 8), pl.ds(8, 8)),
           -1: (pl.ds(RO, 8), pl.ds(RO + ny, 8))}
     gxs = {0: (pl.ds(0, ng), pl.ds(1, ng)), 1: (pl.ds(ng - 1, 1), pl.ds(0, 1)),
@@ -371,7 +371,7 @@
     load_k.wait()
     pl.semaphore_wait(barrier, len(partners))
     k0 = halo_copies(K0, PS0.at[0], PR0.at[0], ssem.at[0], rsem.at[0], n0, me)
-    b0 = halo_copies(B0, PS0.at[1], PR0.at[1], ssem.at[1], rsem.at[1], n0, me)
+    b0 = halo_copies(B0, PS0.at[1], PR0.at[1], ssem.at[1], rsem.at[1], n0, me, HX - 1)
     flat = [o[2] == 0 for o in OFFSETS]
     start([c for c, f in zip(k0, flat) if f])
     pack_z(K0, PS0.at[0], n0)
@@ -477,7 +477,7 @@
     store.start()
     place(B1, resid_wide(n0, (0, 1), 16, 17), n1, HX)
     pack_z(B1, PS1.at[1], n1)
-    b1 = halo_copies(B1, PS1.at[1], PR1.at[1], ssem.at[3], rsem.at[3], n1, me)
+    b1 = halo_copies(B1, PS1.at[1], PR1.at[1], ssem.at[3], rsem.at[3], n1, me, HX - 1)
     start(b1)
     store.wait()
     land(k1, K1, PR1.at[0], n1, True)

time: 68.1 us -> 67.8 us (level)
  no operation moved by 1% of the time
where the time goes in v4:
time: 67.8 us; the launch traced here: 67.7 us
  Pallas kernels  67 us (99%)
    pallas_call x1, Pallas kernels, local(): pl.pallas_call(kernel, out_shape=(jax.ShapeDtypeStruct(right_side.shape,...  65.2 us
    pallas_call x1, Pallas kernels, local(): pl.pallas_call(finish, out_shape=(jax.ShapeDtypeStruct(right_side.shape,...  1.84 us

profile of v4, /device:TPU:1, one launch (start us, length us, event | category | flops | bytes accessed | tf_op | source)
XLA Modules:
  0.0 67.7 jit_solution(8744364794455032789)
XLA Ops:
  0.6 65.2 %down_leg.1 = (f32[32,32,128]{2,1,0:T(8,128)}, f32[1,1,4]{2,1,0:T(1,128)}) custom-call(f32[32,32,128]{2,1,0:T(8,128)} %b_hbm.1, f32[32,32,128]{2,1,0:T(8,128)} %k_hbm.1), custom_call_target="tpu_custom_call" | custom-call | tf_op jit(solution)/shard_map/down_leg/pallas_call | solution.py:567
  65.8 1.8 %finish.1 = (f32[32,32,128]{2,1,0:T(8,128)}, f32[1,1,4]{2,1,0:T(1,128)}) custom-call(f32[32,32,128]{2,1,0:T(8,128)} %get-tuple-element.4.fine, f32[1,1,4]{2,1,0:T(1,128)} %get-tuple-element.5.coarse), custom_call_target="tpu_custom_call" | custom-call | tf_op jit(solution)/shard_map/finish/pallas_call | solution.py:581
